TPU v7x, 32 devices: a whole 2x2x4 slice. The times are simulated.
32 devices in a mesh: feat: 8 (over z, y), cand: 4 (over x, core).
Axes of the slice: x: 2, y: 2, z: 4, core: 2. Of those that a mesh axis runs over, the one named last changes fastest.
Arguments:
- cand_grads: bfloat16 [256, 1048576], P('cand', 'feat'), may hold values from -30 to 30
- val_grads: bfloat16 [64, 1048576], P('cand', 'feat'), may hold values from -30 to 30
- second_moment: float32 [1048576], P('feat'), may hold values from 0.0005 to 1.5
- slot_blocks: int32 [8, 128], replicated, may hold values from 0 to 127, as said below
- slot_seeds: int32 [8, 128], replicated, may hold values from 0 to 1073741823
Outputs:
- scores: float32 [256, 16], P('cand', 'feat')
Inputs may be any that keep to these rules, and one draw needn't show every extreme that they name: `slot_blocks`: each row is a permutation of the input blocks; with L = 128 / (devices of feat), G = (devices of feat) / 8, and o_k = k * G for even k and (k - 1) * G + 1 for odd k, slot k of output block b reads an input block whose index divided by L equals (b / L + o_k) modulo the devices of feat (divisions rounded down).
All inputs are finite; a program needn't handle non-finite values.
Results may differ from a plain program's by a relative error of at most 0.0003.
Values sent between devices are 32-bit elements; how exact they have to be, the bound alone decides.
A program may use at most 128 MiB of HBM per device.

v0:
```python
import math

import jax
import jax.numpy as jnp
from jax import lax
from jax.sharding import PartitionSpec as P

PB = 8192
FEATS = 8192
FB = 64
SLOTS = 8
VPT = 4


def block_signs(seed_val, height, breadth):
    across = lax.broadcasted_iota(jnp.int32, (height, breadth), 0)
    column = lax.broadcasted_iota(jnp.int32, (height, breadth), 1)
    mixed = seed_val ^ across * jnp.int32(73856093) ^ column * jnp.int32(19349663)
    for repeat in range(2):
        mixed = mixed ^ lax.shift_right_logical(mixed, jnp.int32(16))
        mixed = mixed * jnp.int32(73244475)
    mixed = mixed ^ lax.shift_right_logical(mixed, jnp.int32(16))
    return (2 * (mixed & 1) - 1).astype(jnp.float32)


def signs_for(seed_val):
    return block_signs(seed_val, PB, FB)


def squares(features):
    return jnp.sum(features * features, axis=(0, 2))


def body(cand_grads, val_grads, second_moment, slot_blocks, slot_seeds):
    local_blocks = second_moment.shape[0] // PB
    first_block = lax.axis_index("feat") * local_blocks
    groups = FEATS // 128
    per_group = 128 // FB
    factor = 1.0 / math.sqrt(SLOTS * PB)
    ncand = cand_grads.shape[0]
    wide = cand_grads.astype(jnp.float32)
    adam_grads = (
        wide / (jnp.sqrt(0.999 * second_moment[None, :] + 0.001 * wide * wide) + 1e-08)
    ).astype(jnp.bfloat16)
    rows_all = jnp.concatenate([adam_grads, val_grads], axis=0)
    height = rows_all.shape[0]

    def one_block(position, summed):
        segment = lax.dynamic_slice_in_dim(rows_all, position * PB, PB, 1)
        matches = (slot_blocks == first_block + position).astype(jnp.int32)
        seeds_now = jnp.sum(slot_seeds * matches, axis=1)
        matrices = (jax.vmap(signs_for)(seeds_now) * factor).astype(jnp.bfloat16)
        partial_out = jnp.einsum(
            "rp,kpf->rkf", segment, matrices, preferred_element_type=jnp.float32
        )
        placing = matches.astype(jnp.float32).reshape(SLOTS, groups, per_group)
        return summed + jnp.einsum(
            "rkf,kgh->grhf", partial_out, placing, precision=lax.Precision.HIGHEST
        )

    start_sum = jnp.zeros((groups, height, per_group, FB), jnp.float32)
    summed = lax.fori_loop(0, local_blocks, one_block, start_sum)
    mine = lax.psum_scatter(
        summed.reshape(groups, height, 128), "feat", scatter_dimension=0, tiled=True
    )
    cand_part = mine[:, :ncand, :]
    val_part = mine[:, ncand:, :]
    cand_sq, val_sq = lax.psum((squares(cand_part), squares(val_part)), "feat")
    val_unit = val_part / jnp.sqrt(val_sq + 1e-06)[None, :, None]
    val_all = lax.all_gather(val_unit, "cand", axis=1, tiled=True)
    dots = jnp.einsum("gih,gvh->iv", cand_part, val_all, precision=lax.Precision.HIGHEST)
    tile = jnp.sum(dots.reshape(ncand, -1, VPT), axis=2) / VPT
    total = lax.psum(tile, "feat")
    width_own = total.shape[1] // lax.axis_size("feat")
    owned = lax.dynamic_slice_in_dim(total, lax.axis_index("feat") * width_own, width_own, 1)
    cand_norm = jnp.sqrt(cand_sq + 1e-06)
    return owned / cand_norm[:, None]


def solution(mesh):
    placed = (P("cand", "feat"), P("cand", "feat"), P("feat"), P(), P())
    return jax.shard_map(
        body, mesh=mesh, in_specs=placed, out_specs=P("cand", "feat"), check_vma=False
    )
```

profile of v0, /device:TPU:0, one launch (start us, length us, event | category | flops | bytes accessed | tf_op | source)
XLA Modules:
  0.0 469.7 jit_solution(14427390322231028477)
XLA Ops:
  9.2 17.6 %fusion.14 = bf16[64,131072]{1,0:T(8,128)(2,1)S(1)} fusion(bf16[64,131072]{1,0:T(8,128)(2,1)} %param.7, f32[131072]{0:T(1024)S(1)} %broadcast_multiply_fusion), kind=kLoop, calls=%fused_computation.25 | loop fusion | flops 58720256 | bytes 34078720 | tf_op jit(solution)/shard_map/convert_element_type | solution.py:44
  26.8 11.2 %pad_maximum_fusion = bf16[80,131072]{1,0:T(8,128)(2,1)} fusion(bf16[16,131072]{1,0:T(8,128)(2,1)S(1)} %copy-done, bf16[64,131072]{1,0:T(8,128)(2,1)S(1)} %fusion.14), kind=kLoop, calls=%fused_computation.29 | loop fusion | flops 41943040 | bytes 41943040 | tf_op jit(solution)/shard_map/concatenate | solution.py:45
  38.0 298.6 %while.16 = (s32[]{:T(128)}, f32[64,80,2,64]{1,0,3,2:T(8,128)}, s32[]{:T(128)}, s32[8,128]{0,1:T(8,128)S(1)}, bf16[80,131072]{1,0:T(8,128)(2,1)}, /*index=5*/s32...) while((s32[]{:T(128)}, f32[64,80,2,64]{1,0,3,2:T(8,128)}, s32[]{:T(128)}, ...), condition=%wide.region_2.0_spmd.clone, body=%wide.region_0.0_spmd.clone.sunk | while | flops 802436160 | bytes 23841520 | solution.py:62
  38.1 8.3 %fusion.32 = bf16[8,8192,64]{1,2,0:T(8,128)(2,1)S(1)} fusion(s32[64]{0:T(128)S(1)} %iota_multiply_fusion.4, s32[8192]{0:T(1024)S(1)} %iota_multiply_fusion.5, s32[8]{0:T(128)S(1)} %select_reduce_fusion.2), kind=kLoop, calls=%fused_computation.10.clone.1 | loop fusion | flops 67108864 | bytes 8421664 | tf_op jit(solution)/shard_map/while/body/eval_jaxpr/convert_element_type | solution.py:52
  50.1 5.1 %bitcast_add_fusion.2 = f32[64,80,2,64]{1,0,3,2:T(8,128)} fusion(f32[64,80,2,64]{1,0,3,2:T(8,128)} %get-tuple-element.261, pred[]{:T(512)S(6)} %compare.3, f32[80,8,64]{0,2,1:T(8,128)S(1)} %bitcast.32, f32[8,64,2,1]{0,2,1,3:T(2,128)S(1)} %bitcast.33), kind=kOutput, calls=%fused_computation.11.clone.1 | convolution fusion | flops 64225280 | bytes 5410817 | tf_op jit(solution)/shard_map/while/body/eval_jaxpr/rkf,kgh->grhf/dot_general | solution.py:57
  55.3 8.3 %fusion.32 = bf16[8,8192,64]{1,2,0:T(8,128)(2,1)S(1)} fusion(s32[64]{0:T(128)S(1)} %iota_multiply_fusion.4, s32[8192]{0:T(1024)S(1)} %iota_multiply_fusion.5, s32[8]{0:T(128)S(1)} %select_reduce_fusion.2), kind=kLoop, calls=%fused_computation.10.clone.1 | loop fusion | flops 67108864 | bytes 8421664 | tf_op jit(solution)/shard_map/while/body/eval_jaxpr/convert_element_type | solution.py:52
  63.6 3.7 fusion.33
  67.4 6.6 %bitcast_add_fusion.2 = f32[64,80,2,64]{1,0,3,2:T(8,128)} fusion(f32[64,80,2,64]{1,0,3,2:T(8,128)} %get-tuple-element.261, pred[]{:T(512)S(6)} %compare.3, f32[80,8,64]{0,2,1:T(8,128)S(1)} %bitcast.32, f32[8,64,2,1]{0,2,1,3:T(2,128)S(1)} %bitcast.33), kind=kOutput, calls=%fused_computation.11.clone.1 | convolution fusion | flops 64225280 | bytes 5410817 | tf_op jit(solution)/shard_map/while/body/eval_jaxpr/rkf,kgh->grhf/dot_general | solution.py:57
  74.1 8.3 %fusion.32 = bf16[8,8192,64]{1,2,0:T(8,128)(2,1)S(1)} fusion(s32[64]{0:T(128)S(1)} %iota_multiply_fusion.4, s32[8192]{0:T(1024)S(1)} %iota_multiply_fusion.5, s32[8]{0:T(128)S(1)} %select_reduce_fusion.2), kind=kLoop, calls=%fused_computation.10.clone.1 | loop fusion | flops 67108864 | bytes 8421664 | tf_op jit(solution)/shard_map/while/body/eval_jaxpr/convert_element_type | solution.py:52
  82.4 3.7 fusion.33
  86.1 6.6 %bitcast_add_fusion.2 = f32[64,80,2,64]{1,0,3,2:T(8,128)} fusion(f32[64,80,2,64]{1,0,3,2:T(8,128)} %get-tuple-element.261, pred[]{:T(512)S(6)} %compare.3, f32[80,8,64]{0,2,1:T(8,128)S(1)} %bitcast.32, f32[8,64,2,1]{0,2,1,3:T(2,128)S(1)} %bitcast.33), kind=kOutput, calls=%fused_computation.11.clone.1 | convolution fusion | flops 64225280 | bytes 5410817 | tf_op jit(solution)/shard_map/while/body/eval_jaxpr/rkf,kgh->grhf/dot_general | solution.py:57
  92.8 8.3 %fusion.32 = bf16[8,8192,64]{1,2,0:T(8,128)(2,1)S(1)} fusion(s32[64]{0:T(128)S(1)} %iota_multiply_fusion.4, s32[8192]{0:T(1024)S(1)} %iota_multiply_fusion.5, s32[8]{0:T(128)S(1)} %select_reduce_fusion.2), kind=kLoop, calls=%fused_computation.10.clone.1 | loop fusion | flops 67108864 | bytes 8421664 | tf_op jit(solution)/shard_map/while/body/eval_jaxpr/convert_element_type | solution.py:52
  101.2 3.7 fusion.33
  104.9 6.6 %bitcast_add_fusion.2 = f32[64,80,2,64]{1,0,3,2:T(8,128)} fusion(f32[64,80,2,64]{1,0,3,2:T(8,128)} %get-tuple-element.261, pred[]{:T(512)S(6)} %compare.3, f32[80,8,64]{0,2,1:T(8,128)S(1)} %bitcast.32, f32[8,64,2,1]{0,2,1,3:T(2,128)S(1)} %bitcast.33), kind=kOutput, calls=%fused_computation.11.clone.1 | convolution fusion | flops 64225280 | bytes 5410817 | tf_op jit(solution)/shard_map/while/body/eval_jaxpr/rkf,kgh->grhf/dot_general | solution.py:57
  111.6 8.3 %fusion.32 = bf16[8,8192,64]{1,2,0:T(8,128)(2,1)S(1)} fusion(s32[64]{0:T(128)S(1)} %iota_multiply_fusion.4, s32[8192]{0:T(1024)S(1)} %iota_multiply_fusion.5, s32[8]{0:T(128)S(1)} %select_reduce_fusion.2), kind=kLoop, calls=%fused_computation.10.clone.1 | loop fusion | flops 67108864 | bytes 8421664 | tf_op jit(solution)/shard_map/while/body/eval_jaxpr/convert_element_type | solution.py:52
  119.9 3.7 fusion.33
  123.6 6.6 %bitcast_add_fusion.2 = f32[64,80,2,64]{1,0,3,2:T(8,128)} fusion(f32[64,80,2,64]{1,0,3,2:T(8,128)} %get-tuple-element.261, pred[]{:T(512)S(6)} %compare.3, f32[80,8,64]{0,2,1:T(8,128)S(1)} %bitcast.32, f32[8,64,2,1]{0,2,1,3:T(2,128)S(1)} %bitcast.33), kind=kOutput, calls=%fused_computation.11.clone.1 | convolution fusion | flops 64225280 | bytes 5410817 | tf_op jit(solution)/shard_map/while/body/eval_jaxpr/rkf,kgh->grhf/dot_general | solution.py:57
  130.4 8.3 %fusion.32 = bf16[8,8192,64]{1,2,0:T(8,128)(2,1)S(1)} fusion(s32[64]{0:T(128)S(1)} %iota_multiply_fusion.4, s32[8192]{0:T(1024)S(1)} %iota_multiply_fusion.5, s32[8]{0:T(128)S(1)} %select_reduce_fusion.2), kind=kLoop, calls=%fused_computation.10.clone.1 | loop fusion | flops 67108864 | bytes 8421664 | tf_op jit(solution)/shard_map/while/body/eval_jaxpr/convert_element_type | solution.py:52
  138.7 3.7 fusion.33
  142.4 6.6 %bitcast_add_fusion.2 = f32[64,80,2,64]{1,0,3,2:T(8,128)} fusion(f32[64,80,2,64]{1,0,3,2:T(8,128)} %get-tuple-element.261, pred[]{:T(512)S(6)} %compare.3, f32[80,8,64]{0,2,1:T(8,128)S(1)} %bitcast.32, f32[8,64,2,1]{0,2,1,3:T(2,128)S(1)} %bitcast.33), kind=kOutput, calls=%fused_computation.11.clone.1 | convolution fusion | flops 64225280 | bytes 5410817 | tf_op jit(solution)/shard_map/while/body/eval_jaxpr/rkf,kgh->grhf/dot_general | solution.py:57
  149.1 8.3 %fusion.32 = bf16[8,8192,64]{1,2,0:T(8,128)(2,1)S(1)} fusion(s32[64]{0:T(128)S(1)} %iota_multiply_fusion.4, s32[8192]{0:T(1024)S(1)} %iota_multiply_fusion.5, s32[8]{0:T(128)S(1)} %select_reduce_fusion.2), kind=kLoop, calls=%fused_computation.10.clone.1 | loop fusion | flops 67108864 | bytes 8421664 | tf_op jit(solution)/shard_map/while/body/eval_jaxpr/convert_element_type | solution.py:52
  157.5 3.7 fusion.33
  161.2 6.6 %bitcast_add_fusion.2 = f32[64,80,2,64]{1,0,3,2:T(8,128)} fusion(f32[64,80,2,64]{1,0,3,2:T(8,128)} %get-tuple-element.261, pred[]{:T(512)S(6)} %compare.3, f32[80,8,64]{0,2,1:T(8,128)S(1)} %bitcast.32, f32[8,64,2,1]{0,2,1,3:T(2,128)S(1)} %bitcast.33), kind=kOutput, calls=%fused_computation.11.clone.1 | convolution fusion | flops 64225280 | bytes 5410817 | tf_op jit(solution)/shard_map/while/body/eval_jaxpr/rkf,kgh->grhf/dot_general | solution.py:57
  167.9 8.3 %fusion.32 = bf16[8,8192,64]{1,2,0:T(8,128)(2,1)S(1)} fusion(s32[64]{0:T(128)S(1)} %iota_multiply_fusion.4, s32[8192]{0:T(1024)S(1)} %iota_multiply_fusion.5, s32[8]{0:T(128)S(1)} %select_reduce_fusion.2), kind=kLoop, calls=%fused_computation.10.clone.1 | loop fusion | flops 67108864 | bytes 8421664 | tf_op jit(solution)/shard_map/while/body/eval_jaxpr/convert_element_type | solution.py:52
  176.2 3.7 fusion.33
  179.9 6.6 %bitcast_add_fusion.2 = f32[64,80,2,64]{1,0,3,2:T(8,128)} fusion(f32[64,80,2,64]{1,0,3,2:T(8,128)} %get-tuple-element.261, pred[]{:T(512)S(6)} %compare.3, f32[80,8,64]{0,2,1:T(8,128)S(1)} %bitcast.32, f32[8,64,2,1]{0,2,1,3:T(2,128)S(1)} %bitcast.33), kind=kOutput, calls=%fused_computation.11.clone.1 | convolution fusion | flops 64225280 | bytes 5410817 | tf_op jit(solution)/shard_map/while/body/eval_jaxpr/rkf,kgh->grhf/dot_general | solution.py:57
  186.7 8.3 %fusion.32 = bf16[8,8192,64]{1,2,0:T(8,128)(2,1)S(1)} fusion(s32[64]{0:T(128)S(1)} %iota_multiply_fusion.4, s32[8192]{0:T(1024)S(1)} %iota_multiply_fusion.5, s32[8]{0:T(128)S(1)} %select_reduce_fusion.2), kind=kLoop, calls=%fused_computation.10.clone.1 | loop fusion | flops 67108864 | bytes 8421664 | tf_op jit(solution)/shard_map/while/body/eval_jaxpr/convert_element_type | solution.py:52
  195.0 3.7 fusion.33
  198.7 6.6 %bitcast_add_fusion.2 = f32[64,80,2,64]{1,0,3,2:T(8,128)} fusion(f32[64,80,2,64]{1,0,3,2:T(8,128)} %get-tuple-element.261, pred[]{:T(512)S(6)} %compare.3, f32[80,8,64]{0,2,1:T(8,128)S(1)} %bitcast.32, f32[8,64,2,1]{0,2,1,3:T(2,128)S(1)} %bitcast.33), kind=kOutput, calls=%fused_computation.11.clone.1 | convolution fusion | flops 64225280 | bytes 5410817 | tf_op jit(solution)/shard_map/while/body/eval_jaxpr/rkf,kgh->grhf/dot_general | solution.py:57
  205.4 8.3 %fusion.32 = bf16[8,8192,64]{1,2,0:T(8,128)(2,1)S(1)} fusion(s32[64]{0:T(128)S(1)} %iota_multiply_fusion.4, s32[8192]{0:T(1024)S(1)} %iota_multiply_fusion.5, s32[8]{0:T(128)S(1)} %select_reduce_fusion.2), kind=kLoop, calls=%fused_computation.10.clone.1 | loop fusion | flops 67108864 | bytes 8421664 | tf_op jit(solution)/shard_map/while/body/eval_jaxpr/convert_element_type | solution.py:52
  217.5 6.6 %bitcast_add_fusion.2 = f32[64,80,2,64]{1,0,3,2:T(8,128)} fusion(f32[64,80,2,64]{1,0,3,2:T(8,128)} %get-tuple-element.261, pred[]{:T(512)S(6)} %compare.3, f32[80,8,64]{0,2,1:T(8,128)S(1)} %bitcast.32, f32[8,64,2,1]{0,2,1,3:T(2,128)S(1)} %bitcast.33), kind=kOutput, calls=%fused_computation.11.clone.1 | convolution fusion | flops 64225280 | bytes 5410817 | tf_op jit(solution)/shard_map/while/body/eval_jaxpr/rkf,kgh->grhf/dot_general | solution.py:57
  224.2 8.3 %fusion.32 = bf16[8,8192,64]{1,2,0:T(8,128)(2,1)S(1)} fusion(s32[64]{0:T(128)S(1)} %iota_multiply_fusion.4, s32[8192]{0:T(1024)S(1)} %iota_multiply_fusion.5, s32[8]{0:T(128)S(1)} %select_reduce_fusion.2), kind=kLoop, calls=%fused_computation.10.clone.1 | loop fusion | flops 67108864 | bytes 8421664 | tf_op jit(solution)/shard_map/while/body/eval_jaxpr/convert_element_type | solution.py:52
  236.2 6.6 %bitcast_add_fusion.2 = f32[64,80,2,64]{1,0,3,2:T(8,128)} fusion(f32[64,80,2,64]{1,0,3,2:T(8,128)} %get-tuple-element.261, pred[]{:T(512)S(6)} %compare.3, f32[80,8,64]{0,2,1:T(8,128)S(1)} %bitcast.32, f32[8,64,2,1]{0,2,1,3:T(2,128)S(1)} %bitcast.33), kind=kOutput, calls=%fused_computation.11.clone.1 | convolution fusion | flops 64225280 | bytes 5410817 | tf_op jit(solution)/shard_map/while/body/eval_jaxpr/rkf,kgh->grhf/dot_general | solution.py:57
  242.9 8.3 %fusion.32 = bf16[8,8192,64]{1,2,0:T(8,128)(2,1)S(1)} fusion(s32[64]{0:T(128)S(1)} %iota_multiply_fusion.4, s32[8192]{0:T(1024)S(1)} %iota_multiply_fusion.5, s32[8]{0:T(128)S(1)} %select_reduce_fusion.2), kind=kLoop, calls=%fused_computation.10.clone.1 | loop fusion | flops 67108864 | bytes 8421664 | tf_op jit(solution)/shard_map/while/body/eval_jaxpr/convert_element_type | solution.py:52
  255.0 6.6 %bitcast_add_fusion.2 = f32[64,80,2,64]{1,0,3,2:T(8,128)} fusion(f32[64,80,2,64]{1,0,3,2:T(8,128)} %get-tuple-element.261, pred[]{:T(512)S(6)} %compare.3, f32[80,8,64]{0,2,1:T(8,128)S(1)} %bitcast.32, f32[8,64,2,1]{0,2,1,3:T(2,128)S(1)} %bitcast.33), kind=kOutput, calls=%fused_computation.11.clone.1 | convolution fusion | flops 64225280 | bytes 5410817 | tf_op jit(solution)/shard_map/while/body/eval_jaxpr/rkf,kgh->grhf/dot_general | solution.py:57
  261.7 8.3 %fusion.32 = bf16[8,8192,64]{1,2,0:T(8,128)(2,1)S(1)} fusion(s32[64]{0:T(128)S(1)} %iota_multiply_fusion.4, s32[8192]{0:T(1024)S(1)} %iota_multiply_fusion.5, s32[8]{0:T(128)S(1)} %select_reduce_fusion.2), kind=kLoop, calls=%fused_computation.10.clone.1 | loop fusion | flops 67108864 | bytes 8421664 | tf_op jit(solution)/shard_map/while/body/eval_jaxpr/convert_element_type | solution.py:52
  273.7 6.6 %bitcast_add_fusion.2 = f32[64,80,2,64]{1,0,3,2:T(8,128)} fusion(f32[64,80,2,64]{1,0,3,2:T(8,128)} %get-tuple-element.261, pred[]{:T(512)S(6)} %compare.3, f32[80,8,64]{0,2,1:T(8,128)S(1)} %bitcast.32, f32[8,64,2,1]{0,2,1,3:T(2,128)S(1)} %bitcast.33), kind=kOutput, calls=%fused_computation.11.clone.1 | convolution fusion | flops 64225280 | bytes 5410817 | tf_op jit(solution)/shard_map/while/body/eval_jaxpr/rkf,kgh->grhf/dot_general | solution.py:57
  280.5 8.3 %fusion.32 = bf16[8,8192,64]{1,2,0:T(8,128)(2,1)S(1)} fusion(s32[64]{0:T(128)S(1)} %iota_multiply_fusion.4, s32[8192]{0:T(1024)S(1)} %iota_multiply_fusion.5, s32[8]{0:T(128)S(1)} %select_reduce_fusion.2), kind=kLoop, calls=%fused_computation.10.clone.1 | loop fusion | flops 67108864 | bytes 8421664 | tf_op jit(solution)/shard_map/while/body/eval_jaxpr/convert_element_type | solution.py:52
  292.5 6.6 %bitcast_add_fusion.2 = f32[64,80,2,64]{1,0,3,2:T(8,128)} fusion(f32[64,80,2,64]{1,0,3,2:T(8,128)} %get-tuple-element.261, pred[]{:T(512)S(6)} %compare.3, f32[80,8,64]{0,2,1:T(8,128)S(1)} %bitcast.32, f32[8,64,2,1]{0,2,1,3:T(2,128)S(1)} %bitcast.33), kind=kOutput, calls=%fused_computation.11.clone.1 | convolution fusion | flops 64225280 | bytes 5410817 | tf_op jit(solution)/shard_map/while/body/eval_jaxpr/rkf,kgh->grhf/dot_general | solution.py:57
  299.2 8.3 %fusion.32 = bf16[8,8192,64]{1,2,0:T(8,128)(2,1)S(1)} fusion(s32[64]{0:T(128)S(1)} %iota_multiply_fusion.4, s32[8192]{0:T(1024)S(1)} %iota_multiply_fusion.5, s32[8]{0:T(128)S(1)} %select_reduce_fusion.2), kind=kLoop, calls=%fused_computation.10.clone.1 | loop fusion | flops 67108864 | bytes 8421664 | tf_op jit(solution)/shard_map/while/body/eval_jaxpr/convert_element_type | solution.py:52
  311.3 6.6 %bitcast_add_fusion.2 = f32[64,80,2,64]{1,0,3,2:T(8,128)} fusion(f32[64,80,2,64]{1,0,3,2:T(8,128)} %get-tuple-element.261, pred[]{:T(512)S(6)} %compare.3, f32[80,8,64]{0,2,1:T(8,128)S(1)} %bitcast.32, f32[8,64,2,1]{0,2,1,3:T(2,128)S(1)} %bitcast.33), kind=kOutput, calls=%fused_computation.11.clone.1 | convolution fusion | flops 64225280 | bytes 5410817 | tf_op jit(solution)/shard_map/while/body/eval_jaxpr/rkf,kgh->grhf/dot_general | solution.py:57
  318.0 8.3 %fusion.32 = bf16[8,8192,64]{1,2,0:T(8,128)(2,1)S(1)} fusion(s32[64]{0:T(128)S(1)} %iota_multiply_fusion.4, s32[8192]{0:T(1024)S(1)} %iota_multiply_fusion.5, s32[8]{0:T(128)S(1)} %select_reduce_fusion.2), kind=kLoop, calls=%fused_computation.10.clone.1 | loop fusion | flops 67108864 | bytes 8421664 | tf_op jit(solution)/shard_map/while/body/eval_jaxpr/convert_element_type | solution.py:52
  330.0 6.6 %bitcast_add_fusion.2 = f32[64,80,2,64]{1,0,3,2:T(8,128)} fusion(f32[64,80,2,64]{1,0,3,2:T(8,128)} %get-tuple-element.261, pred[]{:T(512)S(6)} %compare.3, f32[80,8,64]{0,2,1:T(8,128)S(1)} %bitcast.32, f32[8,64,2,1]{0,2,1,3:T(2,128)S(1)} %bitcast.33), kind=kOutput, calls=%fused_computation.11.clone.1 | convolution fusion | flops 64225280 | bytes 5410817 | tf_op jit(solution)/shard_map/while/body/eval_jaxpr/rkf,kgh->grhf/dot_general | solution.py:57
  336.7 5.2 %copy.19 = f32[64,80,128]{2,1,0:T(8,128)} copy(f32[64,80,128]{1,0,2:T(8,128)} %bitcast.31) | data formatting | bytes 5242880 | tf_op jit(solution)/shard_map/reshape | solution.py:64
  341.9 73.4 %reduce-scatter.2.cloned.1.call-done = f32[8,80,128]{2,1,0:T(8,128)} async-done(((f32[64,80,128]{2,1,0:T(8,128)}), f32[8,80,128]{2,1,0:T(8,128)}) %reduce-scatter.2.cloned.1.call-update) | async-done | bytes 327696 | tf_op jit(solution)/shard_map/reduce_scatter | solution.py:63
  416.2 19.3 %psum.21 = f32[16]{0:T(128)S(1)} all-reduce(f32[16]{0:T(128)S(1)} %multiply_reduce_fusion.1), channel_id=1, replica_groups=mesh['feat'=8,'cand'=4] {'feat'}, use_global_device_ids=true, to_apply=%region_5.0 | all-reduce | flops 16 | bytes 128 | tf_op jit(solution)/shard_map/psum | solution.py:68
  436.5 5.8 %all_gather.3 = f32[8,64,128]{2,1,0:T(8,128)S(1)} all-gather(f32[8,16,128]{2,1,0:T(8,128)S(1)} %slice_divide_fusion), channel_id=1, replica_groups=mesh['feat'=8,'cand'=4] {'cand'}, dimensions={1}, use_global_device_ids=true | all-gather | bytes 327680 | tf_op jit(solution)/shard_map/all_gather | solution.py:70
  444.7 17.6 %all-reduce = (f32[64,16]{0,1:T(8,128)S(1)}, f32[64]{0:T(128)S(1)}) all-reduce(f32[64,16]{0,1:T(8,128)S(1)} %broadcast_multiply_fusion.1, f32[64]{0:T(128)S(1)} %multiply_reduce_fusion), channel_id=1, replica_groups=mesh['feat'=8,'cand'=4] {'feat'}, use_global_device_ids=true, to_apply=%region_7.0 | all-reduce | flops 1088 | bytes 8704 | tf_op jit(solution)/shard_map/psum | solution.py:73
  (89 shorter events, 38.1 us)
Async XLA Ops:
  6.5 408.7 %reduce-scatter.2.cloned.1.call-start = ((), (), s32[]{:S(2)}) async-start(), calls=%async_computation.1 | async-start | bytes 2949120 | tf_op jit(solution)/shard_map/reduce_scatter | solution.py:63
  9.2 17.6 %copy-start = (bf16[16,131072]{1,0:T(8,128)(2,1)S(1)}, bf16[16,131072]{1,0:T(8,128)(2,1)}, u32[]{:S(2)}) copy-start(bf16[16,131072]{1,0:T(8,128)(2,1)} %param.8) | copy-start | bytes 12582916
Sparse Core Ops, SparseCore 0:
  342.0 73.2 reduce-scatter.1
where the time goes:
time: 471 us; the launch traced here: 470 us
  other arithmetic  168 us (36%)
  matrix products  165 us (35%)
  waiting for transfers between devices  73.4 us (16%)
  blocking collectives  42.7 us (9%)
  between operations  13.5 us (3%)
  local copies, waits for them, and re-layouts  6.73 us (1%)
    convert_element_type x16, other arithmetic, one_block(): matrices = (jax.vmap(signs_for)(seeds_now) * factor).astype(jnp.bfloat16)  133 us
    dot_general x16, matrix products, one_block(): jnp.einsum('rkf,kgh->grhf', partial_out, placing, precision=lax.Precision...  105 us
    reduce_scatter x1, waiting for transfers between devices, body(): lax.psum_scatter(summed.reshape(groups, height, 128), 'feat', scatter_dim...  73.4 us
    while x16, matrix products  59.2 us
    psum x1, blocking collectives, body(): cand_sq, val_sq = lax.psum((squares(cand_part), squares(val_part)), 'feat')  19.3 us
    psum x1, blocking collectives, body(): total = lax.psum(tile, 'feat')  17.6 us
    convert_element_type x1, other arithmetic, body(): adam_grads = (wide / (jnp.sqrt(0.999 * second_moment[None, :] + 0.001 * w...  17.6 us
    concatenate x1, other arithmetic, body(): rows_all = jnp.concatenate([adam_grads, val_grads], axis=0)  11.2 us
  transfers between devices with their start and end apart: 1, of which 1 were waited for; matrix products, arithmetic and copies ran while one was open for 0% of the time, Pallas kernels for 0%

commit v1 on v0

v1 whole, which is shorter than its diff:
```python
import functools
import math

import jax
import jax.numpy as jnp
from jax import lax
from jax.experimental import pallas as pl
from jax.experimental.pallas import tpu as pltpu
from jax.sharding import PartitionSpec as P

PB = 8192
FB = 64
SLOTS = 8
VPT = 4
LANES = 128
MESH = pl.DeviceIdType.MESH
C_ROW = 73856093
C_COL = 19349663
C_MIX = 73244475
C_SIGN = ((C_MIX << 15) + (1 << 31)) & 0xFFFFFFFF
C_SIGN = C_SIGN - (1 << 32) if C_SIGN >= (1 << 31) else C_SIGN
KC = 2048
KS = 256
HIGHEST = lax.Precision.HIGHEST


def fold(h):
    return h ^ lax.shift_right_logical(h, jnp.int32(16))


def slot_shift(k, nf):
    stride = nf // SLOTS
    return k * stride if k % 2 == 0 else (k - 1) * stride + 1


def kernel(
    nf, nc, L,
    blocks_ref, seeds_ref, cand_ref, val_ref, moment_ref, out_ref,
    table, lhs, acc, prev, stage, arrived, mine, val_all, part, part_in,
    send_sem, recv_sem, val_send, val_recv, part_send, part_recv,
):
    j = pl.program_id(0)
    me = lax.axis_index("feat")
    col = lax.axis_index("cand")
    ncand = cand_ref.shape[0]
    nval = val_ref.shape[0]
    rows = ncand + nval

    @pl.when(j == 0)
    def _():
        barrier = pltpu.get_barrier_semaphore()
        for o in range(1, nf):
            pl.semaphore_signal(
                barrier, inc=1, device_id={"feat": lax.rem(me + o, nf)}, device_id_type=MESH
            )
        for o in range(1, nc):
            pl.semaphore_signal(
                barrier, inc=1, device_id={"cand": lax.rem(col + o, nc)}, device_id_type=MESH
            )

        def fill(i, carry):
            base = pl.multiple_of(i * KS, KS)
            p = lax.broadcasted_iota(jnp.int32, (KS, LANES), 0) + base
            f = lax.broadcasted_iota(jnp.int32, (KS, LANES), 1) & (FB - 1)
            table[pl.ds(base, KS), :] = fold((p * jnp.int32(C_ROW)) ^ (f * jnp.int32(C_COL)))
            return carry

        lax.fori_loop(0, PB // KS, fill, 0)

    lane = lax.broadcasted_iota(jnp.int32, (1, LANES), 1)
    low = lane < FB
    pair_seeds = []
    for q in range(SLOTS // 2):
        a = seeds_ref[2 * q, j]
        b = seeds_ref[2 * q + 1, j]
        pair_seeds.append(fold(jnp.where(low, a, b)))

    acc[...] = jnp.zeros_like(acc)

    def chunk(c, carry):
        base = pl.multiple_of(c * KC, KC)
        for s in range(KC // KS):
            here = pl.ds(base + s * KS, KS)
            wide = cand_ref[:, here].astype(jnp.float32)
            u = 0.999 * moment_ref[0, :, here] + 0.001 * (wide * wide)
            root = u * lax.rsqrt(u)
            adam = wide * pl.reciprocal(root + 1e-08, approx=True)
            lhs[:ncand, s * KS:(s + 1) * KS] = adam.astype(jnp.bfloat16)
            lhs[ncand:, s * KS:(s + 1) * KS] = val_ref[:, here]
        for h in range(SLOTS // 4):
            total = None
            for s in range(KC // KS):
                here = pl.ds(base + s * KS, KS)
                sides = []
                for q in (2 * h, 2 * h + 1):
                    x = (table[here, :] ^ pair_seeds[q]) * jnp.int32(C_MIX)
                    g = fold(x) * jnp.int32(C_SIGN)
                    sides.append(jnp.where(g < 0, 1.0, -1.0).astype(jnp.bfloat16))
                signs = jnp.concatenate(sides, axis=1)
                product = jnp.dot(
                    lhs[:, s * KS:(s + 1) * KS], signs, preferred_element_type=jnp.float32
                )
                total = product if total is None else total + product
            acc[:, h * 256:(h + 1) * 256] += total
        return carry

    lax.fori_loop(0, PB // KC, chunk, 0)

    odd = lax.rem(j, 2) == 1

    @pl.when(jnp.logical_not(odd))
    def _():
        prev[...] = acc[...]

    @pl.when(j == 1)
    def _():
        pl.semaphore_wait(pltpu.get_barrier_semaphore(), nf + nc - 2)

    def feature_copy(k, pair):
        return pltpu.make_async_remote_copy(
            src_ref=stage.at[k, pair],
            dst_ref=arrived.at[k, pair],
            send_sem=send_sem.at[k],
            recv_sem=recv_sem.at[k],
            device_id={"feat": lax.rem(me + nf - slot_shift(k, nf), nf)},
            device_id_type=MESH,
        )

    @pl.when(odd)
    def _():
        pair = lax.div(j, 2)
        for q in range(SLOTS // 2):
            first = prev[:, q * LANES:(q + 1) * LANES]
            second = acc[:, q * LANES:(q + 1) * LANES]
            stage[2 * q, pair] = jnp.where(low, first, pltpu.roll(second, FB, 1))
            stage[2 * q + 1, pair] = jnp.where(low, pltpu.roll(first, FB, 1), second)
        for k in range(1, SLOTS):
            feature_copy(k, pair).start()

    @pl.when(j == L - 1)
    def _():
        for k in range(1, SLOTS):
            pltpu.make_async_remote_copy(
                src_ref=stage.at[k],
                dst_ref=arrived.at[k],
                send_sem=send_sem.at[k],
                recv_sem=recv_sem.at[k],
                device_id={"feat": lax.rem(me + nf - slot_shift(k, nf), nf)},
                device_id_type=MESH,
            ).wait()
        factor = 1.0 / math.sqrt(SLOTS * PB)
        for i in range(L // 2):
            total = None
            for k in range(SLOTS):
                j0 = lax.rem(blocks_ref[k, me * L + 2 * i], jnp.int32(L))
                j1 = lax.rem(blocks_ref[k, me * L + 2 * i + 1], jnp.int32(L))
                held = stage if k == 0 else arrived
                x = held[k, lax.shift_right_logical(j0, jnp.int32(1))]
                y = held[k, lax.shift_right_logical(j1, jnp.int32(1))]
                take_x = jnp.broadcast_to(j0 & 1, (1, LANES)) == 0
                take_y = jnp.broadcast_to(j1 & 1, (1, LANES)) == 1
                x = jnp.where(take_x, x, pltpu.roll(x, FB, 1))
                y = jnp.where(take_y, y, pltpu.roll(y, FB, 1))
                both = jnp.where(low, x, y)
                total = both if total is None else total + both
            total = total * factor
            mine[:, i * LANES:(i + 1) * LANES] = total[:ncand]
            val_all[col, :, i * LANES:(i + 1) * LANES] = total[ncand:]

        def val_copy(o):
            return pltpu.make_async_remote_copy(
                src_ref=val_all.at[col],
                dst_ref=val_all.at[col],
                send_sem=val_send.at[o],
                recv_sem=val_recv.at[o],
                device_id={"cand": lax.rem(col + o, nc)},
                device_id_type=MESH,
            )

        for o in range(1, nc):
            val_copy(o).start()
        feats = mine[...]
        ones = jnp.ones((8, L * FB), jnp.float32)
        contract = (((1,), (1,)), ((), ()))
        cand_sq = lax.dot_general(
            ones, feats * feats, contract, precision=HIGHEST, preferred_element_type=jnp.float32
        )
        for o in range(1, nc):
            val_copy(o).wait()
        vals = val_all[...].reshape(nc * nval, L * FB)
        dots = lax.dot_general(
            vals, feats, contract, precision=HIGHEST, preferred_element_type=jnp.float32
        )
        val_sq = jnp.sum(vals * vals, axis=1, keepdims=True)
        vrows = nc * nval // nf
        for t in range(nf):
            here = slice(t * vrows, (t + 1) * vrows)
            part[t, :vrows, :ncand] = dots[here]
            part[t, :vrows, ncand:] = jnp.broadcast_to(val_sq[here], (vrows, LANES - ncand))
            part[t, vrows:, :ncand] = cand_sq
            part[t, vrows:, ncand:] = jnp.zeros((8, LANES - ncand), jnp.float32)

        def part_copy(o):
            to = lax.rem(me + o, nf)
            return pltpu.make_async_remote_copy(
                src_ref=part.at[to],
                dst_ref=part_in.at[o],
                send_sem=part_send.at[o],
                recv_sem=part_recv.at[o],
                device_id={"feat": to},
                device_id_type=MESH,
            )

        for o in range(1, nf):
            part_copy(o).start()
        total = part[me]
        for o in range(1, nf):
            part_copy(o).wait()
            total = total + part_in[o]
        unit = total[:vrows, :ncand] / jnp.sqrt(total[:vrows, ncand:2 * ncand] + 1e-06)
        norm = jnp.sqrt(total[vrows:vrows + 1, :ncand] + 1e-06)
        for t in range(vrows // VPT):
            summed = jnp.sum(unit[t * VPT:(t + 1) * VPT], axis=0, keepdims=True)
            out_ref[t:t + 1, :] = summed / VPT / norm


def body(nf, nc, cand_grads, val_grads, second_moment, slot_blocks, slot_seeds):
    L = second_moment.shape[0] // PB
    ncand, nval = cand_grads.shape[0], val_grads.shape[0]
    rows = ncand + nval
    first = lax.axis_index("feat") * L
    local = first + jnp.arange(L, dtype=jnp.int32)
    matches = slot_blocks[:, None, :] == local[None, :, None]
    seeds = jnp.sum(jnp.where(matches, slot_seeds[:, None, :], 0), axis=2)
    vrows = nc * nval // nf
    f32, bf16, i32 = jnp.float32, jnp.bfloat16, jnp.int32
    VMEM, DMA = pltpu.VMEM, pltpu.SemaphoreType.DMA
    out = pl.pallas_call(
        functools.partial(kernel, nf, nc, L),
        out_shape=jax.ShapeDtypeStruct((vrows // VPT, ncand), f32),
        grid=(L,),
        in_specs=[
            pl.BlockSpec(memory_space=pltpu.SMEM),
            pl.BlockSpec(memory_space=pltpu.SMEM),
            pl.BlockSpec((ncand, PB), lambda j: (0, j)),
            pl.BlockSpec((nval, PB), lambda j: (0, j)),
            pl.BlockSpec((1, 1, PB), lambda j: (j, 0, 0)),
        ],
        out_specs=pl.BlockSpec((vrows // VPT, ncand), lambda j: (0, 0)),
        scratch_shapes=[
            VMEM((PB, LANES), i32),
            VMEM((rows, KC), bf16),
            VMEM((rows, SLOTS * FB), f32),
            VMEM((rows, SLOTS * FB), f32),
            VMEM((SLOTS, L // 2, rows, LANES), f32),
            VMEM((SLOTS, L // 2, rows, LANES), f32),
            VMEM((ncand, L * FB), f32),
            VMEM((nc, nval, L * FB), f32),
            VMEM((nf, vrows + 8, LANES), f32),
            VMEM((nf, vrows + 8, LANES), f32),
            DMA((SLOTS,)), DMA((SLOTS,)),
            DMA((nc,)), DMA((nc,)),
            DMA((nf,)), DMA((nf,)),
        ],
        compiler_params=pltpu.CompilerParams(
            collective_id=0, has_side_effects=True, vmem_limit_bytes=48 * 1024 * 1024,
            dimension_semantics=("arbitrary",),
        ),
        cost_estimate=pl.CostEstimate(
            flops=2 * rows * L * PB * SLOTS * FB, bytes_accessed=2 * rows * L * PB, transcendentals=0
        ),
    )(slot_blocks, seeds, cand_grads, val_grads, second_moment.reshape(L, 1, PB))
    return out.T


def solution(mesh):
    placed = (P("cand", "feat"), P("cand", "feat"), P("feat"), P(), P())
    return jax.shard_map(
        functools.partial(body, mesh.shape["feat"], mesh.shape["cand"]),
        mesh=mesh, in_specs=placed, out_specs=P("cand", "feat"), check_vma=False,
    )
```

time: 471 us -> 119 us (0.25)
  other arithmetic: 168 us -> 0.98 us
  matrix products: 165 us -> 0 us
  Pallas kernels: 0 us -> 113 us
  waiting for transfers between devices: 73.4 us -> 0 us
  blocking collectives: 42.7 us -> 0 us
  between operations: 13.5 us -> 0.03 us
    convert_element_type x33 -> x0, other arithmetic: 151 us -> none  [the longest x16 133 us: one_block(): matrices = (jax.vmap(signs_for)(seeds_now) * factor).astype(jnp.bfloat16)]
    pallas_call x0 -> x1, Pallas kernels: none -> 113 us  [body(): pl.pallas_call(functools.partial(kernel, nf, nc, L), out_shape=jax.ShapeD...]
    dot_general x17 -> x0, matrix products: 106 us -> none  [the longest x16 105 us: one_block(): jnp.einsum('rkf,kgh->grhf', partial_out, placing, precision=lax.Precision...]
    reduce_scatter x1 -> x0, waiting for transfers between devices: 73.4 us -> none  [body(): lax.psum_scatter(summed.reshape(groups, height, 128), 'feat', scatter_dim...]
    while x16 -> x0, matrix products: 59.2 us -> none
    psum x2 -> x0, blocking collectives: 36.9 us -> none  [the longest x1 19.3 us: body(): cand_sq, val_sq = lax.psum((squares(cand_part), squares(val_part)), 'feat')]
    concatenate x1 -> x0, other arithmetic: 11.2 us -> none  [body(): rows_all = jnp.concatenate([adam_grads, val_grads], axis=0)]
    all_gather x1 -> x0, blocking collectives: 5.77 us -> none  [body(): val_all = lax.all_gather(val_unit, 'cand', axis=1, tiled=True)]
  transfers between devices with their start and end apart: 1 -> 0, of which waited for: 1 -> 0; matrix products, arithmetic and copies ran while one was open for 0% -> 0% of each run, Pallas kernels for 0% -> 0%
where the time goes in v1:
time: 119 us
  Pallas kernels  113 us (95%)
  local copies, waits for them, and re-layouts  4.48 us (4%)
    pallas_call x1, Pallas kernels, body(): pl.pallas_call(functools.partial(kernel, nf, nc, L), out_shape=jax.ShapeD...  113 us
    unnamed x7, local copies, waits for them, and re-layouts  4.48 us

profile of v1, /device:TPU:0, one launch (start us, length us, event | category | flops | bytes accessed | tf_op | source)
XLA Modules:
  0.0 118.6 jit_solution(1914365781410937810)
XLA Ops:
  0.0 1.0 select_reduce_fusion.seeds_ref
  1.0 0.0 copy-start
  1.0 0.7 copy-done
  1.7 0.0 copy-start.1
  1.7 2.2 %copy-done.1 = bf16[16,131072]{1,0:T(8,128)(2,1)S(1)} copy-done((bf16[16,131072]{1,0:T(8,128)(2,1)S(1)}, bf16[16,131072]{1,0:T(8,128)(2,1)}, u32[]{:S(2)}) %copy-start.1) | copy-done | bytes 4194328
  3.9 0.0 copy-start.2
  3.9 1.0 copy-done.2
  4.9 113.2 %shard_map.55 = f32[2,64]{1,0:T(2,128)S(1)} custom-call(s32[8,128]{1,0:T(8,128)S(1)} %copy-done, s32[8,16]{1,0:T(8,128)S(1)} %select_reduce_fusion.seeds_ref, bf16[64,131072]{1,0:T(8,128)(2,1)} %cand_ref.1, bf16[16,131072]{1,0:T(8,128)(2,1)S(1)} %copy-done.1, f32[16,1,8192]{2,1,0:T(1,128)S(1)} %bitcast.3), custom_call_target="tpu_custom_call" | custom-call | flops 10737418240 | bytes 20971520 | tf_op jit(solution)/shard_map/pallas_call | solution.py:238
  118.1 0.6 copy.7
  (1 shorter events, 0.0 us)
Async XLA Ops:
  1.0 0.7 copy-start
  1.7 2.2 %copy-start.1 = (bf16[16,131072]{1,0:T(8,128)(2,1)S(1)}, bf16[16,131072]{1,0:T(8,128)(2,1)}, u32[]{:S(2)}) copy-start(bf16[16,131072]{1,0:T(8,128)(2,1)} %val_ref.1) | copy-start | bytes 12582916
  3.9 1.0 copy-start.2

commit v2 on v1

v2 whole, which is shorter than its diff:
```python
import functools
import math

import jax
import jax.numpy as jnp
from jax import lax
from jax.experimental import pallas as pl
from jax.experimental.pallas import tpu as pltpu
from jax.sharding import PartitionSpec as P

PB = 8192
FB = 64
SLOTS = 8
VPT = 4
LANES = 128
MESH = pl.DeviceIdType.MESH
C_ROW = 73856093
C_COL = 19349663
C_MIX = 73244475
C_SIGN = ((C_MIX << 15) + (1 << 31)) & 0xFFFFFFFF
C_SIGN = C_SIGN - (1 << 32) if C_SIGN >= (1 << 31) else C_SIGN
KC = 2048
KS = 256
HIGHEST = lax.Precision.HIGHEST


def fold(h):
    return h ^ lax.shift_right_logical(h, jnp.int32(16))


def slot_shift(k, nf):
    stride = nf // SLOTS
    return k * stride if k % 2 == 0 else (k - 1) * stride + 1


def kernel(
    nf, nc, L,
    blocks_ref, seeds_ref, cand_ref, val_ref, moment_ref, out_ref,
    table, lhs, own, outgoing, incoming, acc, prev, stage, arrived, mine, val_all, part, part_in,
    grad_send, grad_recv, send_sem, recv_sem, val_send, val_recv, part_send, part_recv,
):
    i = pl.program_id(0)
    steps = L // 2
    pairs = L // 4
    me = lax.axis_index("feat")
    col = lax.axis_index("cand")
    core = lax.rem(col, 2)
    other = col + 1 - 2 * core
    ncand = cand_ref.shape[0]
    nval = val_ref.shape[0]
    rows = ncand + nval
    nch = PB // KC

    @pl.when(i == 0)
    def _():
        barrier = pltpu.get_barrier_semaphore()
        for o in range(1, nc):
            pl.semaphore_signal(
                barrier, inc=1, device_id={"cand": lax.rem(col + o, nc)}, device_id_type=MESH
            )
        for o in range(1, nf):
            for c in (col, other):
                pl.semaphore_signal(
                    barrier, inc=1, device_id={"feat": lax.rem(me + o, nf), "cand": c},
                    device_id_type=MESH,
                )

        def fill(r, carry):
            base = pl.multiple_of(r * KS, KS)
            p = lax.broadcasted_iota(jnp.int32, (KS, LANES), 0) + base
            f = lax.broadcasted_iota(jnp.int32, (KS, LANES), 1) & (FB - 1)
            table[pl.ds(base, KS), :] = fold((p * jnp.int32(C_ROW)) ^ (f * jnp.int32(C_COL)))
            return carry

        lax.fori_loop(0, PB // KS, fill, 0)
        pl.semaphore_wait(barrier, 2 * (nf - 1) + nc - 1)

    lane = lax.broadcasted_iota(jnp.int32, (1, LANES), 1)
    low = lane < FB

    def adam_part(block, here):
        at = pl.ds(pl.multiple_of(block * PB + here, KS), KS)
        wide = cand_ref[:, at].astype(jnp.float32)
        u = 0.999 * moment_ref[0, :, at] + 0.001 * (wide * wide)
        root = u * lax.rsqrt(u)
        adam = wide * pl.reciprocal(root + 1e-08, approx=True)
        return adam.astype(jnp.bfloat16), val_ref[:, at]

    def grad_copy(slot, c):
        src = outgoing.at[slot] if c is None else outgoing.at[slot, c]
        dst = incoming.at[i] if c is None else incoming.at[i, c]
        return pltpu.make_async_remote_copy(
            src_ref=src, dst_ref=dst,
            send_sem=grad_send.at[slot], recv_sem=grad_recv.at[i],
            device_id={"cand": other}, device_id_type=MESH,
        )

    def whole_grad(step):
        slot = lax.rem(step, 2)
        return pltpu.make_async_remote_copy(
            src_ref=outgoing.at[slot], dst_ref=incoming.at[step],
            send_sem=grad_send.at[slot], recv_sem=grad_recv.at[step],
            device_id={"cand": other}, device_id_type=MESH,
        )

    def feature_copy(k, t, pair):
        src = stage.at[k, t] if pair is None else stage.at[k, t, pair]
        dst = arrived.at[k, core] if pair is None else arrived.at[k, core, pair]
        to = lax.rem(me + nf - slot_shift(k, nf), nf)
        return pltpu.make_async_remote_copy(
            src_ref=src, dst_ref=dst,
            send_sem=send_sem.at[k, t], recv_sem=recv_sem.at[k, core],
            device_id={"feat": to, "cand": other if t else col}, device_id_type=MESH,
        )

    @pl.when(i < steps)
    def _():
        slot = lax.rem(i, 2)

        @pl.when(i >= 2)
        def _():
            whole_grad(i - 2).wait_send()

        def give(c, carry):
            for s in range(KC // KS):
                here = slice(s * KS, (s + 1) * KS)
                adam, val = adam_part(1 - core, c * KC + s * KS)
                outgoing[slot, c, :ncand, here] = adam.astype(jnp.float32)
                outgoing[slot, c, ncand:, here] = val.astype(jnp.float32)
            grad_copy(slot, c).start()
            return carry

        def keep(c, carry):
            for s in range(KC // KS):
                here = slice(s * KS, (s + 1) * KS)
                adam, val = adam_part(core, c * KC + s * KS)
                own[slot, c, :ncand, here] = adam
                own[slot, c, ncand:, here] = val
            return carry

        lax.fori_loop(0, nch, give, 0)
        lax.fori_loop(0, nch, keep, 0)

    @pl.when(i > 0)
    def _():
        step = i - 1
        block = 2 * step + core
        slot = lax.rem(step, 2)
        pair_seeds = []
        for q in range(SLOTS // 2):
            a = seeds_ref[2 * q, block]
            b = seeds_ref[2 * q + 1, block]
            pair_seeds.append(fold(jnp.where(low, a, b)))

        acc[...] = jnp.zeros_like(acc)
        whole_grad(step).wait_recv()

        def chunk(c, carry):
            base = pl.multiple_of(c * KC, KC)
            lhs[:rows] = own[slot, c]
            lhs[rows:] = incoming[step, c].astype(jnp.bfloat16)
            for h in range(SLOTS // 4):
                total = None
                for s in range(KC // KS):
                    here = pl.ds(base + s * KS, KS)
                    sides = []
                    for q in (2 * h, 2 * h + 1):
                        x = (table[here, :] ^ pair_seeds[q]) * jnp.int32(C_MIX)
                        g = fold(x) * jnp.int32(C_SIGN)
                        sides.append(jnp.where(g < 0, 1.0, -1.0).astype(jnp.bfloat16))
                    signs = jnp.concatenate(sides, axis=1)
                    product = jnp.dot(
                        lhs[:, s * KS:(s + 1) * KS], signs, preferred_element_type=jnp.float32
                    )
                    total = product if total is None else total + product
                acc[:, h * 256:(h + 1) * 256] += total
            return carry

        lax.fori_loop(0, nch, chunk, 0)
        odd = lax.rem(step, 2) == 1

        @pl.when(jnp.logical_not(odd))
        def _():
            prev[...] = acc[...]

        @pl.when(odd)
        def _():
            pair = lax.div(step, 2)
            for q in range(SLOTS // 2):
                first = prev[:, q * LANES:(q + 1) * LANES]
                second = acc[:, q * LANES:(q + 1) * LANES]
                even_slot = jnp.where(low, first, pltpu.roll(second, FB, 1))
                odd_slot = jnp.where(low, pltpu.roll(first, FB, 1), second)
                for k, full in ((2 * q, even_slot), (2 * q + 1, odd_slot)):
                    if k == 0:
                        arrived[k, core, pair] = full[:rows]
                    else:
                        stage[k, 0, pair] = full[:rows]
                    stage[k, 1, pair] = full[rows:]
            for k in range(SLOTS):
                for t in (0, 1):
                    if k or t:
                        feature_copy(k, t, pair).start()

    def feature_wait(k, c):
        pltpu.make_async_remote_copy(
            src_ref=stage.at[k, 1], dst_ref=arrived.at[k, c],
            send_sem=send_sem.at[k, 1], recv_sem=recv_sem.at[k, c],
            device_id={"cand": other}, device_id_type=MESH,
        ).wait_recv()

    @pl.when(i == steps)
    def _():
        whole_grad(steps - 2).wait_send()
        whole_grad(steps - 1).wait_send()
        for k in range(SLOTS):
            for t in (0, 1):
                if k or t:
                    feature_copy(k, t, None).wait_send()
            if k:
                feature_wait(k, core)
            feature_wait(k, 1 - core)
        factor = 1.0 / math.sqrt(SLOTS * PB)
        for i in range(L // 2):
            total = None
            for k in range(SLOTS):
                j0 = lax.rem(blocks_ref[k, me * L + 2 * i], jnp.int32(L))
                j1 = lax.rem(blocks_ref[k, me * L + 2 * i + 1], jnp.int32(L))
                x = arrived[k, j0 & 1, lax.shift_right_logical(j0, jnp.int32(2))]
                y = arrived[k, j1 & 1, lax.shift_right_logical(j1, jnp.int32(2))]
                take_x = jnp.broadcast_to(j0 & 2, (1, LANES)) == 0
                take_y = jnp.broadcast_to(j1 & 2, (1, LANES)) == 2
                x = jnp.where(take_x, x, pltpu.roll(x, FB, 1))
                y = jnp.where(take_y, y, pltpu.roll(y, FB, 1))
                both = jnp.where(low, x, y)
                total = both if total is None else total + both
            total = total * factor
            mine[:, i * LANES:(i + 1) * LANES] = total[:ncand]
            val_all[col, :, i * LANES:(i + 1) * LANES] = total[ncand:]

        def val_copy(o):
            return pltpu.make_async_remote_copy(
                src_ref=val_all.at[col],
                dst_ref=val_all.at[col],
                send_sem=val_send.at[o],
                recv_sem=val_recv.at[o],
                device_id={"cand": lax.rem(col + o, nc)},
                device_id_type=MESH,
            )

        for o in range(1, nc):
            val_copy(o).start()
        feats = mine[...]
        ones = jnp.ones((8, L * FB), jnp.float32)
        contract = (((1,), (1,)), ((), ()))
        cand_sq = lax.dot_general(
            ones, feats * feats, contract, precision=HIGHEST, preferred_element_type=jnp.float32
        )
        for o in range(1, nc):
            val_copy(o).wait()
        vals = val_all[...].reshape(nc * nval, L * FB)
        dots = lax.dot_general(
            vals, feats, contract, precision=HIGHEST, preferred_element_type=jnp.float32
        )
        val_sq = jnp.sum(vals * vals, axis=1, keepdims=True)
        vrows = nc * nval // nf
        for t in range(nf):
            here = slice(t * vrows, (t + 1) * vrows)
            part[t, :vrows, :ncand] = dots[here]
            part[t, :vrows, ncand:] = jnp.broadcast_to(val_sq[here], (vrows, LANES - ncand))
            part[t, vrows:, :ncand] = cand_sq
            part[t, vrows:, ncand:] = jnp.zeros((8, LANES - ncand), jnp.float32)

        def part_copy(o):
            to = lax.rem(me + o, nf)
            return pltpu.make_async_remote_copy(
                src_ref=part.at[to],
                dst_ref=part_in.at[o],
                send_sem=part_send.at[o],
                recv_sem=part_recv.at[o],
                device_id={"feat": to},
                device_id_type=MESH,
            )

        for o in range(1, nf):
            part_copy(o).start()
        total = part[me]
        for o in range(1, nf):
            part_copy(o).wait()
            total = total + part_in[o]
        unit = total[:vrows, :ncand] / jnp.sqrt(total[:vrows, ncand:2 * ncand] + 1e-06)
        norm = jnp.sqrt(total[vrows:vrows + 1, :ncand] + 1e-06)
        for t in range(vrows // VPT):
            summed = jnp.sum(unit[t * VPT:(t + 1) * VPT], axis=0, keepdims=True)
            out_ref[t:t + 1, :] = summed / VPT / norm


def body(nf, nc, cand_grads, val_grads, second_moment, slot_blocks, slot_seeds):
    L = second_moment.shape[0] // PB
    ncand, nval = cand_grads.shape[0], val_grads.shape[0]
    rows = ncand + nval
    first = lax.axis_index("feat") * L
    local = first + jnp.arange(L, dtype=jnp.int32)
    matches = slot_blocks[:, None, :] == local[None, :, None]
    seeds = jnp.sum(jnp.where(matches, slot_seeds[:, None, :], 0), axis=2)
    vrows = nc * nval // nf
    steps = L // 2
    f32, bf16, i32 = jnp.float32, jnp.bfloat16, jnp.int32
    VMEM, DMA = pltpu.VMEM, pltpu.SemaphoreType.DMA
    out = pl.pallas_call(
        functools.partial(kernel, nf, nc, L),
        out_shape=jax.ShapeDtypeStruct((vrows // VPT, ncand), f32),
        grid=(steps + 1,),
        in_specs=[
            pl.BlockSpec(memory_space=pltpu.SMEM),
            pl.BlockSpec(memory_space=pltpu.SMEM),
            pl.BlockSpec((ncand, 2 * PB), lambda i: (0, jnp.minimum(i, steps - 1))),
            pl.BlockSpec((nval, 2 * PB), lambda i: (0, jnp.minimum(i, steps - 1))),
            pl.BlockSpec((1, 1, 2 * PB), lambda i: (jnp.minimum(i, steps - 1), 0, 0)),
        ],
        out_specs=pl.BlockSpec((vrows // VPT, ncand), lambda i: (0, 0)),
        scratch_shapes=[
            VMEM((PB, LANES), i32),
            VMEM((2 * rows, KC), bf16),
            VMEM((2, PB // KC, rows, KC), bf16),
            VMEM((2, PB // KC, rows, KC), f32),
            VMEM((steps, PB // KC, rows, KC), f32),
            VMEM((2 * rows, SLOTS * FB), f32),
            VMEM((2 * rows, SLOTS * FB), f32),
            VMEM((SLOTS, 2, L // 4, rows, LANES), f32),
            VMEM((SLOTS, 2, L // 4, rows, LANES), f32),
            VMEM((ncand, L * FB), f32),
            VMEM((nc, nval, L * FB), f32),
            VMEM((nf, vrows + 8, LANES), f32),
            VMEM((nf, vrows + 8, LANES), f32),
            DMA((2,)), DMA((steps,)),
            DMA((SLOTS, 2)), DMA((SLOTS, 2)),
            DMA((nc,)), DMA((nc,)),
            DMA((nf,)), DMA((nf,)),
        ],
        compiler_params=pltpu.CompilerParams(
            collective_id=0, has_side_effects=True, vmem_limit_bytes=56 * 1024 * 1024,
            dimension_semantics=("arbitrary",),
        ),
        cost_estimate=pl.CostEstimate(
            flops=2 * rows * L * PB * SLOTS * FB, bytes_accessed=2 * rows * L * PB, transcendentals=0
        ),
    )(slot_blocks, seeds, cand_grads, val_grads, second_moment.reshape(steps, 1, 2 * PB))
    return out.T


def solution(mesh):
    placed = (P("cand", "feat"), P("cand", "feat"), P("feat"), P(), P())
    return jax.shard_map(
        functools.partial(body, mesh.shape["feat"], mesh.shape["cand"]),
        mesh=mesh, in_specs=placed, out_specs=P("cand", "feat"), check_vma=False,
    )
```

time: 119 us -> 95.8 us (0.81)
  Pallas kernels: 113 us -> 92.8 us
  local copies, waits for them, and re-layouts: 4.48 us -> 1.22 us
    pallas_call x1, Pallas kernels: 113 us -> 92.8 us  [body(): pl.pallas_call(functools.partial(kernel, nf, nc, L), out_shape=jax.ShapeD...]
    unnamed x7 -> x1, local copies, waits for them, and re-layouts: 4.48 us -> 1.22 us
where the time goes in v2:
time: 95.8 us; the launch traced here: 95.6 us
  Pallas kernels  92.8 us (97%)
  other arithmetic  1.58 us (2%)
  local copies, waits for them, and re-layouts  1.22 us (1%)
    pallas_call x1, Pallas kernels, body(): pl.pallas_call(functools.partial(kernel, nf, nc, L), out_shape=jax.ShapeD...  92.8 us

profile of v2, /device:TPU:0, one launch (start us, length us, event | category | flops | bytes accessed | tf_op | source)
XLA Modules:
  0.0 95.6 jit_solution(7707177489782489274)
XLA Ops:
  0.0 1.6 %select_reduce_fusion.seeds_ref = s32[8,16]{1,0:T(8,128)} fusion(s32[8,128]{1,0:T(8,128)} %param.9, s32[8,128]{1,0:T(8,128)} %blocks_ref.1, s32[16]{0:T(128)S(1)} %iota_add_fusion), kind=kLoop, calls=%fused_computation | loop fusion | flops 49024 | bytes 8768 | tf_op jit(solution)/shard_map/reduce_sum | solution.py:305
  1.6 92.8 %shard_map.55 = f32[2,64]{1,0:T(2,128)} custom-call(s32[8,128]{1,0:T(8,128)} %blocks_ref.1, s32[8,16]{1,0:T(8,128)} %select_reduce_fusion.seeds_ref, bf16[64,131072]{1,0:T(8,128)(2,1)} %cand_ref.1, bf16[16,131072]{1,0:T(8,128)(2,1)} %val_ref.1, f32[8,1,16384]{2,1,0:T(1,128)} %bitcast.3), custom_call_target="tpu_custom_call" | custom-call | flops 10737418240 | bytes 20971520 | tf_op jit(solution)/shard_map/pallas_call | solution.py:310
  94.3 1.2 %copy.7 = f32[64,2]{0,1:T(2,128)} copy(f32[64,2]{0,1:T(2,128)} %bitcast.2) | data formatting | bytes 1024
  (1 shorter events, 0.0 us)

commit v3 on v2

--- a/solution.py
+++ b/solution.py
@@ -35,13 +35,12 @@
 
 def kernel(
     nf, nc, L,
-    blocks_ref, seeds_ref, cand_ref, val_ref, moment_ref, out_ref,
-    table, lhs, own, outgoing, incoming, acc, prev, stage, arrived, mine, val_all, part, part_in,
+    blocks_ref, map_ref, seeds_ref, cand_ref, val_ref, moment_ref, out_ref,
+    table, lhs, own, outgoing, incoming, acc, stage, arrived, mine, val_all, part, part_in,
     grad_send, grad_recv, send_sem, recv_sem, val_send, val_recv, part_send, part_recv,
 ):
     i = pl.program_id(0)
     steps = L // 2
-    pairs = L // 4
     me = lax.axis_index("feat")
     col = lax.axis_index("cand")
     core = lax.rem(col, 2)
@@ -65,14 +64,6 @@
                     device_id_type=MESH,
                 )
 
-        def fill(r, carry):
-            base = pl.multiple_of(r * KS, KS)
-            p = lax.broadcasted_iota(jnp.int32, (KS, LANES), 0) + base
-            f = lax.broadcasted_iota(jnp.int32, (KS, LANES), 1) & (FB - 1)
-            table[pl.ds(base, KS), :] = fold((p * jnp.int32(C_ROW)) ^ (f * jnp.int32(C_COL)))
-            return carry
-
-        lax.fori_loop(0, PB // KS, fill, 0)
         pl.semaphore_wait(barrier, 2 * (nf - 1) + nc - 1)
 
     lane = lax.broadcasted_iota(jnp.int32, (1, LANES), 1)
@@ -86,12 +77,11 @@
         adam = wide * pl.reciprocal(root + 1e-08, approx=True)
         return adam.astype(jnp.bfloat16), val_ref[:, at]
 
-    def grad_copy(slot, c):
-        src = outgoing.at[slot] if c is None else outgoing.at[slot, c]
-        dst = incoming.at[i] if c is None else incoming.at[i, c]
+    def grad_copy(step, c):
+        slot = lax.rem(step, 2)
         return pltpu.make_async_remote_copy(
-            src_ref=src, dst_ref=dst,
-            send_sem=grad_send.at[slot], recv_sem=grad_recv.at[i],
+            src_ref=outgoing.at[slot, c], dst_ref=incoming.at[step, c],
+            send_sem=grad_send.at[slot], recv_sem=grad_recv.at[step, c],
             device_id={"cand": other}, device_id_type=MESH,
         )
 
@@ -99,7 +89,7 @@
         slot = lax.rem(step, 2)
         return pltpu.make_async_remote_copy(
             src_ref=outgoing.at[slot], dst_ref=incoming.at[step],
-            send_sem=grad_send.at[slot], recv_sem=grad_recv.at[step],
+            send_sem=grad_send.at[slot], recv_sem=grad_recv.at[step, 0],
             device_id={"cand": other}, device_id_type=MESH,
         )
 
@@ -127,7 +117,7 @@
                 adam, val = adam_part(1 - core, c * KC + s * KS)
                 outgoing[slot, c, :ncand, here] = adam.astype(jnp.float32)
                 outgoing[slot, c, ncand:, here] = val.astype(jnp.float32)
-            grad_copy(slot, c).start()
+            grad_copy(i, c).start()
             return carry
 
         def keep(c, carry):
@@ -139,6 +129,18 @@
             return carry
 
         lax.fori_loop(0, nch, give, 0)
+
+        @pl.when(i == 0)
+        def _():
+            def fill(r, carry):
+                base = pl.multiple_of(r * KS, KS)
+                p = lax.broadcasted_iota(jnp.int32, (KS, LANES), 0) + base
+                f = lax.broadcasted_iota(jnp.int32, (KS, LANES), 1) & (FB - 1)
+                table[pl.ds(base, KS), :] = fold((p * jnp.int32(C_ROW)) ^ (f * jnp.int32(C_COL)))
+                return carry
+
+            lax.fori_loop(0, PB // KS, fill, 0)
+
         lax.fori_loop(0, nch, keep, 0)
 
     @pl.when(i > 0)
@@ -146,20 +148,24 @@
         step = i - 1
         block = 2 * step + core
         slot = lax.rem(step, 2)
+        found = map_ref[...] == me * L + block
+        picked = jnp.sum(jnp.where(found, seeds_ref[...], 0), axis=1, keepdims=True)
+        picked = jnp.broadcast_to(picked, (SLOTS, LANES))
         pair_seeds = []
         for q in range(SLOTS // 2):
-            a = seeds_ref[2 * q, block]
-            b = seeds_ref[2 * q + 1, block]
+            a = picked[2 * q:2 * q + 1]
+            b = picked[2 * q + 1:2 * q + 2]
             pair_seeds.append(fold(jnp.where(low, a, b)))
 
         acc[...] = jnp.zeros_like(acc)
-        whole_grad(step).wait_recv()
-
-        def chunk(c, carry):
-            base = pl.multiple_of(c * KC, KC)
-            lhs[:rows] = own[slot, c]
-            lhs[rows:] = incoming[step, c].astype(jnp.bfloat16)
-            for h in range(SLOTS // 4):
+
+        for h in range(SLOTS // 4):
+            def chunk(c, carry):
+                base = pl.multiple_of(c * KC, KC)
+                if h == 0:
+                    grad_copy(step, c).wait_recv()
+                    lhs[c, :rows] = own[slot, c]
+                    lhs[c, rows:] = incoming[step, c].astype(jnp.bfloat16)
                 total = None
                 for s in range(KC // KS):
                     here = pl.ds(base + s * KS, KS)
@@ -170,37 +176,30 @@
                         sides.append(jnp.where(g < 0, 1.0, -1.0).astype(jnp.bfloat16))
                     signs = jnp.concatenate(sides, axis=1)
                     product = jnp.dot(
-                        lhs[:, s * KS:(s + 1) * KS], signs, preferred_element_type=jnp.float32
+                        lhs[c, :, s * KS:(s + 1) * KS], signs, preferred_element_type=jnp.float32
                     )
                     total = product if total is None else total + product
                 acc[:, h * 256:(h + 1) * 256] += total
-            return carry
-
-        lax.fori_loop(0, nch, chunk, 0)
-        odd = lax.rem(step, 2) == 1
-
-        @pl.when(jnp.logical_not(odd))
-        def _():
-            prev[...] = acc[...]
-
-        @pl.when(odd)
-        def _():
-            pair = lax.div(step, 2)
-            for q in range(SLOTS // 2):
-                first = prev[:, q * LANES:(q + 1) * LANES]
-                second = acc[:, q * LANES:(q + 1) * LANES]
-                even_slot = jnp.where(low, first, pltpu.roll(second, FB, 1))
-                odd_slot = jnp.where(low, pltpu.roll(first, FB, 1), second)
-                for k, full in ((2 * q, even_slot), (2 * q + 1, odd_slot)):
-                    if k == 0:
-                        arrived[k, core, pair] = full[:rows]
-                    else:
-                        stage[k, 0, pair] = full[:rows]
-                    stage[k, 1, pair] = full[rows:]
-            for k in range(SLOTS):
+                return carry
+
+            lax.fori_loop(0, nch, chunk, 0)
+            for q in (2 * h, 2 * h + 1):
+                both = acc[:, q * LANES:(q + 1) * LANES]
+                turned = pltpu.roll(both, FB, 1)
+                for t in (0, 1):
+                    top = slice(t * rows, t * rows + rows // 2)
+                    end = slice(t * rows + rows // 2, (t + 1) * rows)
+                    even_slot = jnp.where(low, both[top], turned[end])
+                    odd_slot = jnp.where(low, turned[top], both[end])
+                    for k, folded in ((2 * q, even_slot), (2 * q + 1, odd_slot)):
+                        if k or t:
+                            stage[k, t, step] = folded
+                        else:
+                            arrived[k, core, step] = folded
+            for k in range(4 * h, 4 * h + 4):
                 for t in (0, 1):
                     if k or t:
-                        feature_copy(k, t, pair).start()
+                        feature_copy(k, t, step).start()
 
     def feature_wait(k, c):
         pltpu.make_async_remote_copy(
@@ -221,22 +220,21 @@
                 feature_wait(k, core)
             feature_wait(k, 1 - core)
         factor = 1.0 / math.sqrt(SLOTS * PB)
-        for i in range(L // 2):
-            total = None
-            for k in range(SLOTS):
-                j0 = lax.rem(blocks_ref[k, me * L + 2 * i], jnp.int32(L))
-                j1 = lax.rem(blocks_ref[k, me * L + 2 * i + 1], jnp.int32(L))
-                x = arrived[k, j0 & 1, lax.shift_right_logical(j0, jnp.int32(2))]
-                y = arrived[k, j1 & 1, lax.shift_right_logical(j1, jnp.int32(2))]
-                take_x = jnp.broadcast_to(j0 & 2, (1, LANES)) == 0
-                take_y = jnp.broadcast_to(j1 & 2, (1, LANES)) == 2
-                x = jnp.where(take_x, x, pltpu.roll(x, FB, 1))
-                y = jnp.where(take_y, y, pltpu.roll(y, FB, 1))
-                both = jnp.where(low, x, y)
-                total = both if total is None else total + both
-            total = total * factor
-            mine[:, i * LANES:(i + 1) * LANES] = total[:ncand]
-            val_all[col, :, i * LANES:(i + 1) * LANES] = total[ncand:]
+        for n in range(L // 2):
+            sums = []
+            for b in (2 * n, 2 * n + 1):
+                total = None
+                for k in range(SLOTS):
+                    at = lax.rem(blocks_ref[k, me * L + b], jnp.int32(L))
+                    term = arrived[k, at & 1, lax.shift_right_logical(at, jnp.int32(1))]
+                    total = term if total is None else total + term
+                sums.append(total * factor)
+            top = jnp.where(low, sums[0], pltpu.roll(sums[1], FB, 1))
+            end = jnp.where(low, pltpu.roll(sums[0], FB, 1), sums[1])
+            here = slice(n * LANES, (n + 1) * LANES)
+            mine[:rows // 2, here] = top
+            mine[rows // 2:, here] = end[:ncand - rows // 2]
+            val_all[col, :, here] = end[ncand - rows // 2:]
 
         def val_copy(o):
             return pltpu.make_async_remote_copy(
@@ -299,10 +297,6 @@
     L = second_moment.shape[0] // PB
     ncand, nval = cand_grads.shape[0], val_grads.shape[0]
     rows = ncand + nval
-    first = lax.axis_index("feat") * L
-    local = first + jnp.arange(L, dtype=jnp.int32)
-    matches = slot_blocks[:, None, :] == local[None, :, None]
-    seeds = jnp.sum(jnp.where(matches, slot_seeds[:, None, :], 0), axis=2)
     vrows = nc * nval // nf
     steps = L // 2
     f32, bf16, i32 = jnp.float32, jnp.bfloat16, jnp.int32
@@ -313,7 +307,8 @@
         grid=(steps + 1,),
         in_specs=[
             pl.BlockSpec(memory_space=pltpu.SMEM),
-            pl.BlockSpec(memory_space=pltpu.SMEM),
+            pl.BlockSpec(slot_blocks.shape, lambda i: (0, 0)),
+            pl.BlockSpec(slot_seeds.shape, lambda i: (0, 0)),
             pl.BlockSpec((ncand, 2 * PB), lambda i: (0, jnp.minimum(i, steps - 1))),
             pl.BlockSpec((nval, 2 * PB), lambda i: (0, jnp.minimum(i, steps - 1))),
             pl.BlockSpec((1, 1, 2 * PB), lambda i: (jnp.minimum(i, steps - 1), 0, 0)),
@@ -321,19 +316,18 @@
         out_specs=pl.BlockSpec((vrows // VPT, ncand), lambda i: (0, 0)),
         scratch_shapes=[
             VMEM((PB, LANES), i32),
-            VMEM((2 * rows, KC), bf16),
+            VMEM((PB // KC, 2 * rows, KC), bf16),
             VMEM((2, PB // KC, rows, KC), bf16),
             VMEM((2, PB // KC, rows, KC), f32),
             VMEM((steps, PB // KC, rows, KC), f32),
             VMEM((2 * rows, SLOTS * FB), f32),
-            VMEM((2 * rows, SLOTS * FB), f32),
-            VMEM((SLOTS, 2, L // 4, rows, LANES), f32),
-            VMEM((SLOTS, 2, L // 4, rows, LANES), f32),
+            VMEM((SLOTS, 2, steps, rows // 2, LANES), f32),
+            VMEM((SLOTS, 2, steps, rows // 2, LANES), f32),
             VMEM((ncand, L * FB), f32),
             VMEM((nc, nval, L * FB), f32),
             VMEM((nf, vrows + 8, LANES), f32),
             VMEM((nf, vrows + 8, LANES), f32),
-            DMA((2,)), DMA((steps,)),
+            DMA((2,)), DMA((steps, PB // KC)),
             DMA((SLOTS, 2)), DMA((SLOTS, 2)),
             DMA((nc,)), DMA((nc,)),
             DMA((nf,)), DMA((nf,)),
@@ -345,7 +339,7 @@
         cost_estimate=pl.CostEstimate(
             flops=2 * rows * L * PB * SLOTS * FB, bytes_accessed=2 * rows * L * PB, transcendentals=0
         ),
-    )(slot_blocks, seeds, cand_grads, val_grads, second_moment.reshape(steps, 1, 2 * PB))
+    )(slot_blocks, slot_blocks, slot_seeds, cand_grads, val_grads, second_moment.reshape(steps, 1, 2 * PB))
     return out.T
 
 

time: 95.8 us -> 88 us (0.919)
  Pallas kernels: 92.8 us -> 86.6 us
  other arithmetic: 1.58 us -> 0 us
    pallas_call x1, Pallas kernels: 92.8 us -> 86.6 us  [body(): pl.pallas_call(functools.partial(kernel, nf, nc, L), out_shape=jax.ShapeD...]
    reduce_sum x1 -> x0, other arithmetic: 1.58 us -> none  [body(): seeds = jnp.sum(jnp.where(matches, slot_seeds[:, None, :], 0), axis=2)]
where the time goes in v3:
time: 88 us; the launch traced here: 87.9 us
  Pallas kernels  86.6 us (98%)
  local copies, waits for them, and re-layouts  1.24 us (1%)
    pallas_call x1, Pallas kernels, body(): pl.pallas_call(functools.partial(kernel, nf, nc, L), out_shape=jax.ShapeD...  86.6 us

profile of v3, /device:TPU:0, one launch (start us, length us, event | category | flops | bytes accessed | tf_op | source)
XLA Modules:
  0.0 87.9 jit_solution(472599569253674340)
XLA Ops:
  0.0 86.6 %shard_map.55 = f32[2,64]{1,0:T(2,128)} custom-call(s32[8,128]{1,0:T(8,128)} %map_ref.1, s32[8,128]{1,0:T(8,128)} %map_ref.1, s32[8,128]{1,0:T(8,128)} %seeds_ref.1, bf16[64,131072]{1,0:T(8,128)(2,1)} %cand_ref.1, bf16[16,131072]{1,0:T(8,128)(2,1)} %val_ref.1, f32[8,1,16384]{2,1,0:T(1,128)} %bitcast.3), custom_call_target="tpu_custom_call" | custom-call | flops 10737418240 | bytes 20971520 | tf_op jit(solution)/shard_map/pallas_call | solution.py:304
  86.6 1.2 %copy.7 = f32[64,2]{0,1:T(2,128)} copy(f32[64,2]{0,1:T(2,128)} %bitcast.2) | data formatting | bytes 1024

commit v4 on v3

--- a/solution.py
+++ b/solution.py
@@ -111,24 +111,19 @@
         def _():
             whole_grad(i - 2).wait_send()
 
-        def give(c, carry):
+        def prepare(c, carry):
             for s in range(KC // KS):
                 here = slice(s * KS, (s + 1) * KS)
                 adam, val = adam_part(1 - core, c * KC + s * KS)
                 outgoing[slot, c, :ncand, here] = adam.astype(jnp.float32)
                 outgoing[slot, c, ncand:, here] = val.astype(jnp.float32)
-            grad_copy(i, c).start()
-            return carry
-
-        def keep(c, carry):
-            for s in range(KC // KS):
-                here = slice(s * KS, (s + 1) * KS)
                 adam, val = adam_part(core, c * KC + s * KS)
                 own[slot, c, :ncand, here] = adam
                 own[slot, c, ncand:, here] = val
+            grad_copy(i, c).start()
             return carry
 
-        lax.fori_loop(0, nch, give, 0)
+        lax.fori_loop(0, nch, prepare, 0)
 
         @pl.when(i == 0)
         def _():
@@ -141,7 +136,6 @@
 
             lax.fori_loop(0, PB // KS, fill, 0)
 
-        lax.fori_loop(0, nch, keep, 0)
 
     @pl.when(i > 0)
     def _():
@@ -157,18 +151,19 @@
             b = picked[2 * q + 1:2 * q + 2]
             pair_seeds.append(fold(jnp.where(low, a, b)))
 
-        acc[...] = jnp.zeros_like(acc)
-
-        for h in range(SLOTS // 4):
-            def chunk(c, carry):
-                base = pl.multiple_of(c * KC, KC)
-                if h == 0:
-                    grad_copy(step, c).wait_recv()
-                    lhs[c, :rows] = own[slot, c]
-                    lhs[c, rows:] = incoming[step, c].astype(jnp.bfloat16)
+        def gather(c, carry):
+            grad_copy(step, c).wait_recv()
+            lhs[c, :rows] = own[slot, c]
+            lhs[c, rows:] = incoming[step, c].astype(jnp.bfloat16)
+            return carry
+
+        lax.fori_loop(0, nch, gather, 0)
+
+        for h in reversed(range(SLOTS // 4)):
+            for c in range(nch):
                 total = None
                 for s in range(KC // KS):
-                    here = pl.ds(base + s * KS, KS)
+                    here = pl.ds(c * KC + s * KS, KS)
                     sides = []
                     for q in (2 * h, 2 * h + 1):
                         x = (table[here, :] ^ pair_seeds[q]) * jnp.int32(C_MIX)
@@ -179,10 +174,11 @@
                         lhs[c, :, s * KS:(s + 1) * KS], signs, preferred_element_type=jnp.float32
                     )
                     total = product if total is None else total + product
-                acc[:, h * 256:(h + 1) * 256] += total
-                return carry
-
-            lax.fori_loop(0, nch, chunk, 0)
+                here = slice(h * 256, (h + 1) * 256)
+                if c == 0:
+                    acc[:, here] = total
+                else:
+                    acc[:, here] += total
             for q in (2 * h, 2 * h + 1):
                 both = acc[:, q * LANES:(q + 1) * LANES]
                 turned = pltpu.roll(both, FB, 1)

time: 88 us -> 86.3 us (0.981)
  Pallas kernels: 86.6 us -> 84.9 us
    pallas_call x1, Pallas kernels: 86.6 us -> 84.9 us  [body(): pl.pallas_call(functools.partial(kernel, nf, nc, L), out_shape=jax.ShapeD...]
where the time goes in v4:
time: 86.3 us; the launch traced here: 86.2 us
  Pallas kernels  84.9 us (98%)
  local copies, waits for them, and re-layouts  1.24 us (1%)
    pallas_call x1, Pallas kernels, body(): pl.pallas_call(functools.partial(kernel, nf, nc, L), out_shape=jax.ShapeD...  84.9 us

profile of v4, /device:TPU:0, one launch (start us, length us, event | category | flops | bytes accessed | tf_op | source)
XLA Modules:
  0.0 86.2 jit_solution(9116618595676555620)
XLA Ops:
  0.0 84.9 %shard_map.55 = f32[2,64]{1,0:T(2,128)} custom-call(s32[8,128]{1,0:T(8,128)} %map_ref.1, s32[8,128]{1,0:T(8,128)} %map_ref.1, s32[8,128]{1,0:T(8,128)} %seeds_ref.1, bf16[64,131072]{1,0:T(8,128)(2,1)} %cand_ref.1, bf16[16,131072]{1,0:T(8,128)(2,1)} %val_ref.1, f32[8,1,16384]{2,1,0:T(1,128)} %bitcast.3), custom_call_target="tpu_custom_call" | custom-call | flops 10737418240 | bytes 20971520 | tf_op jit(solution)/shard_map/pallas_call | solution.py:300
  85.0 1.2 %copy.7 = f32[64,2]{0,1:T(2,128)} copy(f32[64,2]{0,1:T(2,128)} %bitcast.2) | data formatting | bytes 1024

commit v5 on v4

--- a/solution.py
+++ b/solution.py
@@ -36,7 +36,7 @@
 def kernel(
     nf, nc, L,
     blocks_ref, map_ref, seeds_ref, cand_ref, val_ref, moment_ref, out_ref,
-    table, lhs, own, outgoing, incoming, acc, stage, arrived, mine, val_all, part, part_in,
+    table, lhs, own, outgoing, incoming, signs, acc, stage, arrived, mine, val_all, part, part_in,
     grad_send, grad_recv, send_sem, recv_sem, val_send, val_recv, part_send, part_recv,
 ):
     i = pl.program_id(0)
@@ -161,19 +161,16 @@
 
         for h in reversed(range(SLOTS // 4)):
             for c in range(nch):
-                total = None
                 for s in range(KC // KS):
-                    here = pl.ds(c * KC + s * KS, KS)
-                    sides = []
-                    for q in (2 * h, 2 * h + 1):
-                        x = (table[here, :] ^ pair_seeds[q]) * jnp.int32(C_MIX)
+                    here = slice(s * KS, (s + 1) * KS)
+                    rows_here = pl.ds(c * KC + s * KS, KS)
+                    for n, q in enumerate((2 * h, 2 * h + 1)):
+                        x = (table[rows_here, :] ^ pair_seeds[q]) * jnp.int32(C_MIX)
                         g = fold(x) * jnp.int32(C_SIGN)
-                        sides.append(jnp.where(g < 0, 1.0, -1.0).astype(jnp.bfloat16))
-                    signs = jnp.concatenate(sides, axis=1)
-                    product = jnp.dot(
-                        lhs[c, :, s * KS:(s + 1) * KS], signs, preferred_element_type=jnp.float32
-                    )
-                    total = product if total is None else total + product
+                        signs[c % 2, here, n * LANES:(n + 1) * LANES] = jnp.where(
+                            g < 0, 1.0, -1.0
+                        ).astype(jnp.bfloat16)
+                total = jnp.dot(lhs[c], signs[c % 2], preferred_element_type=jnp.float32)
                 here = slice(h * 256, (h + 1) * 256)
                 if c == 0:
                     acc[:, here] = total
@@ -316,6 +313,7 @@
             VMEM((2, PB // KC, rows, KC), bf16),
             VMEM((2, PB // KC, rows, KC), f32),
             VMEM((steps, PB // KC, rows, KC), f32),
+            VMEM((2, KC, 2 * LANES), bf16),
             VMEM((2 * rows, SLOTS * FB), f32),
             VMEM((SLOTS, 2, steps, rows // 2, LANES), f32),
             VMEM((SLOTS, 2, steps, rows // 2, LANES), f32),

time: 86.3 us -> 98.9 us (1.15)
  Pallas kernels: 84.9 us -> 97.5 us
    pallas_call x1, Pallas kernels: 84.9 us -> 97.5 us  [body(): pl.pallas_call(functools.partial(kernel, nf, nc, L), out_shape=jax.ShapeD...]
where the time goes in v5:
time: 98.9 us; the launch traced here: 98.8 us
  Pallas kernels  97.5 us (99%)
  local copies, waits for them, and re-layouts  1.24 us (1%)
    pallas_call x1, Pallas kernels, body(): pl.pallas_call(functools.partial(kernel, nf, nc, L), out_shape=jax.ShapeD...  97.5 us

profile of v5, /device:TPU:0, one launch (start us, length us, event | category | flops | bytes accessed | tf_op | source)
XLA Modules:
  0.0 98.8 jit_solution(17351841564046240652)
XLA Ops:
  0.0 97.5 %shard_map.55 = f32[2,64]{1,0:T(2,128)} custom-call(s32[8,128]{1,0:T(8,128)} %map_ref.1, s32[8,128]{1,0:T(8,128)} %map_ref.1, s32[8,128]{1,0:T(8,128)} %seeds_ref.1, bf16[64,131072]{1,0:T(8,128)(2,1)} %cand_ref.1, bf16[16,131072]{1,0:T(8,128)(2,1)} %val_ref.1, f32[8,1,16384]{2,1,0:T(1,128)} %bitcast.3), custom_call_target="tpu_custom_call" | custom-call | flops 10737418240 | bytes 20971520 | tf_op jit(solution)/shard_map/pallas_call | solution.py:297
  97.5 1.2 %copy.7 = f32[64,2]{0,1:T(2,128)} copy(f32[64,2]{0,1:T(2,128)} %bitcast.2) | data formatting | bytes 1024

commit v6 on v4

--- a/solution.py
+++ b/solution.py
@@ -20,7 +20,7 @@
 C_SIGN = ((C_MIX << 15) + (1 << 31)) & 0xFFFFFFFF
 C_SIGN = C_SIGN - (1 << 32) if C_SIGN >= (1 << 31) else C_SIGN
 KC = 2048
-KS = 256
+KS = 512
 HIGHEST = lax.Precision.HIGHEST
 
 

time: 86.3 us -> 86.3 us (level)
  no operation moved by 1% of the time
where the time goes in v6:
time: 86.3 us; the launch traced here: 86.2 us
  Pallas kernels  84.9 us (98%)
  local copies, waits for them, and re-layouts  1.24 us (1%)
    pallas_call x1, Pallas kernels, body(): pl.pallas_call(functools.partial(kernel, nf, nc, L), out_shape=jax.ShapeD...  84.9 us

profile of v6, /device:TPU:0, one launch (start us, length us, event | category | flops | bytes accessed | tf_op | source)
XLA Modules:
  0.0 86.2 jit_solution(5000960720825777242)
XLA Ops:
  0.0 84.9 %shard_map.55 = f32[2,64]{1,0:T(2,128)} custom-call(s32[8,128]{1,0:T(8,128)} %map_ref.1, s32[8,128]{1,0:T(8,128)} %map_ref.1, s32[8,128]{1,0:T(8,128)} %seeds_ref.1, bf16[64,131072]{1,0:T(8,128)(2,1)} %cand_ref.1, bf16[16,131072]{1,0:T(8,128)(2,1)} %val_ref.1, f32[8,1,16384]{2,1,0:T(1,128)} %bitcast.3), custom_call_target="tpu_custom_call" | custom-call | flops 10737418240 | bytes 20971520 | tf_op jit(solution)/shard_map/pallas_call | solution.py:300
  85.0 1.2 %copy.7 = f32[64,2]{0,1:T(2,128)} copy(f32[64,2]{0,1:T(2,128)} %bitcast.2) | data formatting | bytes 1024
